TPU v7x, 32 devices: a whole 2x2x4 slice. The times are simulated.
32 devices in a mesh: grp: 2 (over y), az: 4 (over z), sec: 2 (over core), sub: 2 (over x).
Axes of the slice: x: 2, y: 2, z: 4, core: 2. Of those that a mesh axis runs over, the one named last changes fastest.
Arguments:
- echoes: bfloat16 [2, 4096, 32768], P(None, ('grp', 'az', 'sec'), 'sub'), parts along dimension 1, may hold values from -6 to 6
- chirp_taps: float32 [2, 2048], replicated, may hold values from -0.09375 to 0.09375
- replicas: bfloat16 [2, 1024, 65536], P(None, None, ('grp', 'az', 'sec', 'sub')), parts along dimension 2, may hold values from -0.125 to 0.125
- lengths: int32 [65536], P(('grp', 'az', 'sec', 'sub')), parts along dimension 0, may hold values from 128 to 1024, as said below
Outputs:
- focused: bfloat16 [2, 2048, 65536], P(None, None, ('grp', 'az', 'sec', 'sub')), parts along dimension 2
There are 2 independent parts, one for each index of `grp`. A program takes and returns all parts, laid end to end along the dimension named above; an argument that names none is the same for every part. Nothing has to cross between parts.
Inputs may be any that keep to these rules, and one draw needn't show every extreme that they name: `lengths`: count of the leading taps of each range bin's azimuth replica that belong to it.
All inputs are finite; a program needn't handle non-finite values.
Results may differ from a plain program's by a relative error of at most 0.013.
Values may be sent and summed in bfloat16 or wider, within the bound.
A program may use at most 320 MiB of HBM per device.

v0:
```python
import math

import jax
import jax.numpy as jnp
from jax import lax
from jax.sharding import PartitionSpec as P

R1 = 256
R2 = 128
A1 = 32
A2 = 64
CHIRP = 2048
TAPS = 1024
RANGE = 32768
PULSES = 2048


EXACT_PRECISION = lax.Precision.HIGHEST


def dft_table(length, direction, value_type):
    positions = jnp.arange(length, dtype=jnp.int32)
    phases = positions[:, None] * positions[None, :] % length
    angles = direction * 2.0 * math.pi / length * phases.astype(jnp.float32)
    return (jnp.cos(angles).astype(value_type), jnp.sin(angles).astype(value_type))


def block_table(length, direction):
    cosine, sine = dft_table(length, direction, jnp.bfloat16)
    return jnp.stack([jnp.stack([cosine, sine]), jnp.stack([-sine, cosine])])


def twiddles(rows_count, cols_count, length, direction):
    first_side = jnp.arange(rows_count, dtype=jnp.int32)
    second = jnp.arange(cols_count, dtype=jnp.int32)
    phases = first_side[:, None] * second[None, :] % length
    angles = direction * 2.0 * math.pi / length * phases.astype(jnp.float32)
    return (jnp.cos(angles), jnp.sin(angles))


def exact_mix(pattern, left_real, left_imag, right_real, right_imag):

    def single(left_side, right_side):
        return jnp.einsum(pattern, left_side, right_side, precision=EXACT_PRECISION)

    return (
        single(left_real, right_real) - single(left_imag, right_imag),
        single(left_real, right_imag) + single(left_imag, right_real),
    )


def product(first_real, first_imag, second_real, second_imag):
    return (
        first_real * second_real - first_imag * second_imag,
        first_real * second_imag + first_imag * second_real,
    )


def rotate(stacked, turn_real, turn_imag):
    real_part, imag_part = product(stacked[0], stacked[1], turn_real, turn_imag)
    return jnp.stack([real_part, imag_part])


def apply_table(pattern, stacked, table):
    return jnp.einsum(pattern, stacked, table, preferred_element_type=jnp.float32)


def chirp_spectrum(taps_real, taps_imag, lead_rows):
    padded_real = taps_real.reshape(lead_rows, R2)
    padded_imag = taps_imag.reshape(lead_rows, R2)
    table_real, table_imag = dft_table(R1, -1.0, jnp.float32)
    step_real, step_imag = exact_mix(
        "ab,ak->kb", padded_real, padded_imag, table_real[:lead_rows], table_imag[:lead_rows]
    )
    turn_real, turn_imag = twiddles(R1, R2, RANGE, -1.0)
    step_real, step_imag = product(step_real, step_imag, turn_real, turn_imag)
    second_real, second_imag = dft_table(R2, -1.0, jnp.float32)
    return exact_mix("kb,bm->km", step_real, step_imag, second_real, second_imag)


def range_rows(stacked_rows, filter_real, filter_imag):
    row_count = stacked_rows.shape[1]
    grid = stacked_rows.reshape(2, row_count, R1, R2)
    turn_fwd = twiddles(R1, R2, RANGE, -1.0)
    turn_inv = twiddles(R1, R2, RANGE, 1.0)
    step = apply_table("srab,stak->trkb", grid, block_table(R1, -1.0))
    step = rotate(step, turn_fwd[0], turn_fwd[1]).astype(jnp.bfloat16)
    spec = apply_table("srkb,stbm->trkm", step, block_table(R2, -1.0))
    spec = rotate(spec, filter_real, filter_imag).astype(jnp.bfloat16)
    back = apply_table("srkm,stmd->trkd", spec, block_table(R2, 1.0))
    back = rotate(back, turn_inv[0], turn_inv[1]).astype(jnp.bfloat16)
    out = apply_table("srkd,stkc->trcd", back, block_table(R1, 1.0))
    return out.astype(jnp.bfloat16).reshape(2, row_count, RANGE)


def replica_spectrum(replica_taps, counts, lead_rows):
    bin_count = replica_taps.shape[2]
    kept_taps = jnp.arange(TAPS, dtype=jnp.int32)[:, None] < counts[None, :]
    taps_kept = jnp.where(kept_taps[None], replica_taps, jnp.zeros_like(replica_taps))
    grid = taps_kept.reshape(2, lead_rows, A2, bin_count)
    first_table = block_table(A1, -1.0)[:, :, :lead_rows, :]
    step = apply_table("sabn,stak->tkbn", grid, first_table)
    turn_real, turn_imag = twiddles(A1, A2, PULSES, -1.0)
    step = rotate(step, turn_real[:, :, None], turn_imag[:, :, None]).astype(jnp.bfloat16)
    return apply_table("skbn,stbm->tkmn", step, block_table(A2, -1.0))


def focus_bins(columns, spectrum):
    bin_count = columns.shape[2]
    grid = columns.reshape(2, A1, A2, bin_count)
    turn_fwd = twiddles(A1, A2, PULSES, -1.0)
    turn_inv = twiddles(A1, A2, PULSES, 1.0)
    step = apply_table("sabn,stak->tkbn", grid, block_table(A1, -1.0))
    step = rotate(step, turn_fwd[0][:, :, None], turn_fwd[1][:, :, None]).astype(jnp.bfloat16)
    freq = apply_table("skbn,stbm->tkmn", step, block_table(A2, -1.0))
    freq = rotate(freq, spectrum[0], -spectrum[1])
    scale_factor = 1.0 / PULSES
    freq = (freq * scale_factor).astype(jnp.bfloat16)
    back = apply_table("skmn,stmd->tkdn", freq, block_table(A2, 1.0))
    back = rotate(back, turn_inv[0][:, :, None], turn_inv[1][:, :, None]).astype(jnp.bfloat16)
    out = apply_table("skdn,stkc->tcdn", back, block_table(A1, 1.0))
    return out.astype(jnp.bfloat16).reshape(2, PULSES, bin_count)


def body(echoes, chirp_taps, replicas, lengths):
    chirp_lead = CHIRP // R2
    replica_lead = TAPS // A2
    spec_real, spec_imag = chirp_spectrum(chirp_taps[0], chirp_taps[1], chirp_lead)
    filter_real = spec_real / RANGE
    filter_imag = -spec_imag / RANGE
    sub_count = lax.axis_size("sub")
    pulse_rows = echoes.shape[1]
    sectioned = echoes.reshape(2, sub_count, pulse_rows // sub_count, echoes.shape[2])
    compressed = range_rows(
        lax.all_to_all(sectioned, "sub", split_axis=1, concat_axis=3, tiled=True)[:, 0],
        filter_real,
        filter_imag,
    )
    own_rows = compressed.shape[1]
    spectrum = replica_spectrum(replicas, lengths, replica_lead)
    outer_count = lax.axis_size(("az", "sec"))
    blocks = compressed.reshape(
        2, 1, 1, own_rows, outer_count, sub_count, RANGE // (outer_count * sub_count)
    )
    turned = lax.all_to_all(
        lax.all_to_all(blocks, ("az", "sec"), split_axis=4, concat_axis=1, tiled=True),
        "sub",
        split_axis=5,
        concat_axis=2,
        tiled=True,
    )
    columns = turned.reshape(2, PULSES, turned.shape[-1])
    return focus_bins(columns, spectrum)


def solution(mesh):
    placed = (
        P(None, ("grp", "az", "sec"), "sub"),
        P(),
        P(None, None, ("grp", "az", "sec", "sub")),
        P(("grp", "az", "sec", "sub")),
    )
    return jax.shard_map(
        body,
        mesh=mesh,
        in_specs=placed,
        out_specs=P(None, None, ("grp", "az", "sec", "sub")),
        check_vma=False,
    )
```

profile of v0, /device:TPU:0, one launch (start us, length us, event | category | flops | bytes accessed | tf_op | source)
XLA Modules:
  0.0 1321.7 jit_solution(13833142416077824976)
XLA Ops:
  0.0 30.7 %copy.90 = bf16[2,256,16384]{2,0,1:T(2,128)(2,1)} copy(bf16[2,256,16384]{2,1,0:T(8,128)(2,1)} %param.4) | data formatting | bytes 33554432 | tf_op args[0]
  30.7 9.9 all-to-all-start
  41.7 0.4 convolution_add_fusion.1
  42.5 1.0 fusion.89
  43.6 1.0 fusion.40
  44.7 1.0 fusion.91
  45.7 1.0 fusion.41
  46.9 0.5 multiply_cosine_fusion
  47.5 0.5 multiply_sine_fusion
  49.2 1.0 fusion.77
  50.2 1.0 fusion.76
  51.2 1.4 sine_convert_fusion
  52.6 0.5 multiply_sine_fusion.1
  53.1 1.1 sine_convert_fusion.1
  54.3 170.0 %all-to-all-done = bf16[2,2,128,16384]{3,0,2,1:T(2,128)(2,1)} async-done(((bf16[2,2,128,16384]{3,0,2,1:T(2,128)(2,1)}), bf16[2,2,128,16384]{3,0,2,1:T(2,128)(2,1)}, u32[]{:S(2)}, u32[]{:S(2)}) %all-to-all-start) | async-done | bytes 16777248 | tf_op jit(solution)/shard_map/all_to_all | solution.py:135
  224.3 30.9 %copy.91 = bf16[2,1,128,2,16384]{4,3,0,2,1:T(2,128)(2,1)} copy(bf16[2,1,128,2,16384]{4,0,2,3,1:T(2,128)(2,1)} %bitcast.34) | data formatting | bytes 33554432 | tf_op jit(solution)/shard_map/all_to_all | solution.py:135
  255.2 27.9 %reshape.644 = bf16[2,128,256,128,1]{3,2,0,1,4:T(8,128)(2,1)} reshape(bf16[2,1,128,2,16384]{4,3,0,2,1:T(2,128)(2,1)} %copy.91) | data formatting | bytes 33554432 | tf_op jit(solution)/shard_map/reshape;squeeze | solution.py:83
  283.2 21.1 %convolution_bitcast_fusion = f32[2,128,256,128]{3,2,1,0:T(8,128)} fusion(bf16[2,128,256,128,1]{3,2,0,1,4:T(8,128)(2,1)} %reshape.644, bf16[1,2,256,256]{2,3,0,1:T(8,128)(2,1)S(1)} %get-tuple-element.22, bf16[1,2,256,256]{2,3,0,1:T(8,128)(2,1)S(1)} %get-tuple-element.21), kind=kOutput, calls=%fused_computation.4 | convolution fusion | flops 8590983168 | bytes 50855936 | tf_op jit(solution)/shard_map/srab,stak->trkb/dot_general | solution.py:65
  304.3 14.9 %subtract_convert_fusion.5 = (bf16[1,128,256,128]{3,2,1,0:T(8,128)(2,1)S(1)}, bf16[1,128,256,128]{3,2,1,0:T(8,128)(2,1)}) fusion(f32[2,128,256,128]{3,2,1,0:T(8,128)} %convolution_bitcast_fusion, f32[256,128]{1,0:T(8,128)S(1)} %get-tuple-element.43, f32[256,128]{1,0:T(8,128)S(1)} %get-tuple-element.44), kind=kLoop, calls=%fused_computation.46 | loop fusion | flops 33554432 | bytes 50593792 | tf_op jit(solution)/shard_map/convert.10
  319.1 14.9 %convolution_bitcast_fusion.2 = f32[2,128,256,128]{2,3,1,0:T(8,128)} fusion(bf16[1,2,128,128]{2,3,0,1:T(8,128)(2,1)S(1)} %get-tuple-element.28, bf16[1,2,128,128]{2,3,0,1:T(8,128)(2,1)S(1)} %get-tuple-element.27, bf16[1,128,256,128]{3,2,1,0:T(8,128)(2,1)} %get-tuple-element.12, bf16[1,128,256,128]{3,2,1,0:T(8,128)(2,1)S(1)} %get-tuple-element.11), kind=kOutput, calls=%fused_computation.6 | convolution fusion | flops 4303618048 | bytes 50462720 | tf_op jit(solution)/shard_map/srkb,stbm->trkm/dot_general | solution.py:65
  334.0 17.4 %subtract_convert_fusion.4 = (bf16[1,128,256,128]{2,3,1,0:T(8,128)(2,1)}, bf16[1,128,256,128]{2,3,1,0:T(8,128)(2,1)}) fusion(f32[2,128,256,128]{2,3,1,0:T(8,128)} %convolution_bitcast_fusion.2, f32[256,128]{0,1:T(8,128)S(1)} %copy.94, f32[256,128]{0,1:T(8,128)S(1)} %copy.93), kind=kLoop, calls=%fused_computation.44 | loop fusion | flops 33554432 | bytes 50593792 | tf_op jit(solution)/shard_map/convert.8
  351.4 25.9 %convolution_bitcast_fusion.1 = f32[2,128,256,128]{2,3,1,0:T(8,128)} fusion(bf16[1,128,256,128]{2,3,1,0:T(8,128)(2,1)} %get-tuple-element.10, bf16[1,128,256,128]{2,3,1,0:T(8,128)(2,1)} %get-tuple-element.9, bf16[1,2,128,128]{2,3,1,0:T(8,128)(2,1)S(1)} %get-tuple-element.26, bf16[1,2,128,128]{2,3,1,0:T(8,128)(2,1)S(1)} %get-tuple-element.25), kind=kOutput, calls=%fused_computation.5 | convolution fusion | flops 4303421440 | bytes 50462720 | tf_op jit(solution)/shard_map/srkm,stmd->trkd/dot_general | solution.py:65
  377.3 15.3 %subtract_convert_fusion.3 = (bf16[1,128,256,128]{2,3,1,0:T(8,128)(2,1)S(1)}, bf16[1,128,256,128]{2,3,1,0:T(8,128)(2,1)}) fusion(f32[2,128,256,128]{2,3,1,0:T(8,128)} %convolution_bitcast_fusion.1, f32[256,128]{0,1:T(8,128)S(1)} %copy.98, f32[256,128]{0,1:T(8,128)S(1)} %copy.97), kind=kLoop, calls=%fused_computation.42 | loop fusion | flops 33554432 | bytes 50593792 | tf_op jit(solution)/shard_map/convert.6
  392.6 14.5 %fusion.32 = bf16[2,128,256,128]{3,2,1,0:T(8,128)(2,1)} fusion(bf16[1,128,256,128]{2,3,1,0:T(8,128)(2,1)} %get-tuple-element.8, bf16[1,128,256,128]{2,3,1,0:T(8,128)(2,1)S(1)} %get-tuple-element.7, bf16[1,2,256,256]{2,3,1,0:T(8,128)(2,1)S(1)} %get-tuple-element.20, bf16[1,2,256,256]{2,3,1,0:T(8,128)(2,1)S(1)} %get-tuple-element.19), kind=kOutput, calls=%fused_computation.52 | convolution fusion | flops 8606973952 | bytes 34078720 | tf_op jit(solution)/shard_map/srkd,stkc->trcd/dot_general | solution.py:65
  407.1 23.8 %reshape_reshape.6 = bf16[2,1,1,128,8,2,2048]{6,5,4,3,0,2,1:T(2,128)(2,1)} reshape(bf16[2,128,256,128]{3,2,1,0:T(8,128)(2,1)} %fusion.32) | data formatting | bytes 33554432 | tf_op jit(solution)/shard_map/reshape;reshape | solution.py:142
  430.8 12.2 copy.101
  443.0 369.3 %all_to_all.48 = bf16[2,1,1,128,8,2,2048]{6,3,5,0,2,1,4:T(8,128)(2,1)S(1)} all-to-all(bf16[2,1,1,128,8,2,2048]{6,3,5,0,2,1,4:T(8,128)(2,1)S(1)} %copy.101), channel_id=1, replica_groups=mesh['grp'=2,'az'=4,'sec'=2,'sub'=2] {'az','sec'}, dimensions={4} | all-to-all | bytes 33554432 | tf_op jit(solution)/shard_map/all_to_all | solution.py:146
  812.3 6.5 copy.102
  818.8 9.8 all-to-all-start.2
  830.0 0.7 multiply_sine_fusion.2
  830.7 0.6 maximum_bitcast_fusion.25
  831.4 1.7 iota_compare_fusion
  833.1 7.9 broadcast_select_fusion
  841.0 33.0 %convolution_bitcast_fusion.3 = f32[2,32,64,2048]{3,1,2,0:T(8,128)} fusion(bf16[2,16,64,2048]{3,2,1,0:T(8,128)(2,1)} %bitcast.197, bf16[1,2,32,32]{2,3,0,1:T(8,128)(2,1)S(1)} %get-tuple-element.37, bf16[1,2,32,32]{2,3,0,1:T(8,128)(2,1)S(1)} %get-tuple-element.38), kind=kOutput, calls=%fused_computation.51 | convolution fusion | flops 536879104 | bytes 41951232 | tf_op jit(solution)/shard_map/sabn,stak->tkbn/dot_general | solution.py:65
  874.0 136.8 %all-to-all-done.2 = bf16[2,8,1,128,1,2,2048]{6,3,1,0,4,2,5:T(8,128)(2,1)} async-done(((bf16[2,8,1,128,1,2,2048]{6,3,1,0,4,2,5:T(8,128)(2,1)}), bf16[2,8,1,128,1,2,2048]{6,3,1,0,4,2,5:T(8,128)(2,1)}, u32[]{:S(2)}, u32[]{:S(2)}) %all-to-all-start.2) | async-done | bytes 16777248 | tf_op jit(solution)/shard_map/all_to_all | solution.py:145
  1010.8 14.2 %copy.103 = bf16[2,8,1,128,1,2,2048]{6,3,5,1,0,4,2:T(8,128)(2,1)} copy(bf16[2,8,1,128,1,2,2048]{6,3,1,0,4,2,5:T(8,128)(2,1)} %all-to-all-done.2) | data formatting | bytes 33554432 | tf_op jit(solution)/shard_map/all_to_all | solution.py:145
  1025.0 36.3 %fusion.20 = f32[2,32,64,2048]{3,1,2,0:T(8,128)} fusion(bf16[2,32,64,2048]{3,2,1,0:T(8,128)(2,1)} %bitcast.196, bf16[1,2,32,32]{2,3,0,1:T(8,128)(2,1)S(1)} %get-tuple-element.38, bf16[1,2,32,32]{2,3,0,1:T(8,128)(2,1)S(1)} %get-tuple-element.37), kind=kOutput, calls=%fused_computation.47 | convolution fusion | flops 1073758208 | bytes 50339840 | tf_op jit(solution)/shard_map/sabn,stak->tkbn/dot_general | solution.py:65
  1061.3 34.1 %subtract_convert_fusion.1 = (bf16[1,32,64,2048]{3,1,2,0:T(8,128)(2,1)}, bf16[1,32,64,2048]{3,1,2,0:T(8,128)(2,1)}, bf16[1,32,64,2048]{3,1,2,0:T(8,128)(2,1)}, bf16[1,32,64,2048]{3,1,2,0:T(8,128)(2,1)}) fusion(f32[2,32,64,2048]{3,1,2,0:T(8,128)} %convolution_bitcast_fusion.3, f32[32,64]{0,1:T(8,128)S(1)} %copy.106, f32[32,64]{0,1:T(8,128)S(1)} %copy.105, ...), kind=kLoop, calls=%fused_computation.38 | loop fusion | flops 67108864 | bytes 100679680 | tf_op jit(solution)/shard_map/convert.2
  1095.4 16.2 %pad_maximum_fusion.2 = bf16[2,32,64,2048]{3,1,2,0:T(8,128)(2,1)} fusion(bf16[1,32,64,2048]{3,1,2,0:T(8,128)(2,1)} %get-tuple-element.14, bf16[1,32,64,2048]{3,1,2,0:T(8,128)(2,1)} %get-tuple-element.13), kind=kLoop, calls=%fused_computation.12 | loop fusion | flops 8388608 | bytes 33554432 | tf_op jit(solution)/shard_map/stack | solution.py:61
  1111.6 6.7 pad_maximum_fusion.1
  1118.4 36.2 %fusion.26 = f32[2,32,64,2048]{3,2,1,0:T(8,128)} fusion(bf16[2,32,64,2048]{3,1,2,0:T(8,128)(2,1)} %pad_maximum_fusion.2, bf16[1,2,64,64]{2,3,0,1:T(8,128)(2,1)S(1)} %get-tuple-element.32, bf16[1,2,64,64]{2,3,0,1:T(8,128)(2,1)S(1)} %get-tuple-element.31), kind=kOutput, calls=%fused_computation.49 | convolution fusion | flops 2147549184 | bytes 50364416 | tf_op jit(solution)/shard_map/skbn,stbm->tkmn/dot_general | solution.py:65
  1154.6 36.1 %fusion.23 = f32[2,32,64,2048]{3,2,1,0:T(8,128)} fusion(bf16[2,32,64,2048]{3,1,2,0:T(8,128)(2,1)} %pad_maximum_fusion.1, bf16[1,2,64,64]{2,3,0,1:T(8,128)(2,1)S(1)} %get-tuple-element.32, bf16[1,2,64,64]{2,3,0,1:T(8,128)(2,1)S(1)} %get-tuple-element.31), kind=kOutput, calls=%fused_computation.48 | convolution fusion | flops 2147549184 | bytes 50364416 | tf_op jit(solution)/shard_map/skbn,stbm->tkmn/dot_general | solution.py:65
  1190.7 34.1 %multiply_subtract_fusion = (f32[1,32,64,2048]{3,2,1,0:T(8,128)}, f32[1,32,64,2048]{3,2,1,0:T(8,128)}) fusion(f32[2,32,64,2048]{3,2,1,0:T(8,128)} %fusion.23, f32[2,32,64,2048]{3,2,1,0:T(8,128)} %fusion.26), kind=kLoop, calls=%fused_computation.36 | loop fusion | flops 29360128 | bytes 100663296 | tf_op jit(solution)/shard_map/sub | solution.py:54
  1224.9 24.6 %fusion.29 = f32[2,32,64,2048]{3,2,1,0:T(8,128)} fusion(f32[1,32,64,2048]{3,2,1,0:T(8,128)} %get-tuple-element.6, f32[1,32,64,2048]{3,2,1,0:T(8,128)} %get-tuple-element.5, bf16[1,2,64,64]{2,3,1,0:T(8,128)(2,1)S(1)} %get-tuple-element.30, bf16[1,2,64,64]{2,3,1,0:T(8,128)(2,1)S(1)} %get-tuple-element.29), kind=kOutput, calls=%fused_computation.50 | convolution fusion | flops 2172665856 | bytes 67141632 | tf_op jit(solution)/shard_map/skmn,stmd->tkdn/dot_general | solution.py:65
  1249.5 13.0 subtract_convert_fusion
  1262.5 6.8 pad_maximum_fusion.3
  1269.3 33.4 %bitcast_convert_fusion = bf16[2,32,64,2048]{3,1,2,0:T(8,128)(2,1)} fusion(bf16[2,32,64,2048]{3,2,1,0:T(8,128)(2,1)} %pad_maximum_fusion.3, bf16[1,2,32,32]{2,3,1,0:T(8,128)(2,1)S(1)} %copy-done.3, bf16[1,2,32,32]{2,3,1,0:T(8,128)(2,1)S(1)} %copy-done.2), kind=kOutput, calls=%fused_computation.2 | convolution fusion | flops 1082134528 | bytes 33562624 | tf_op jit(solution)/shard_map/skdn,stkc->tcdn/dot_general | solution.py:65
  1302.7 18.6 %copy.115 = bf16[2,32,64,2048]{3,2,1,0:T(8,128)(2,1)} copy(bf16[2,32,64,2048]{3,1,2,0:T(8,128)(2,1)} %bitcast_convert_fusion) | data formatting | bytes 33554432 | tf_op jit(solution)/shard_map/convert_element_type | solution.py:122
  (48 shorter events, 4.4 us)
Async XLA Ops:
  30.7 10.0 copy-start.6
  30.7 193.6 %all-to-all-start = ((bf16[2,2,128,16384]{3,0,2,1:T(2,128)(2,1)}), bf16[2,2,128,16384]{3,0,2,1:T(2,128)(2,1)}, u32[]{:S(2)}, u32[]{:S(2)}) async-start(bf16[2,2,128,16384]{3,0,2,1:T(2,128)(2,1)} %bitcast.194), calls=%async_computation | async-start | bytes 33554432 | tf_op jit(solution)/shard_map/all_to_all | solution.py:135
  818.8 12.6 copy-start.7
  818.8 192.0 %all-to-all-start.2 = ((bf16[2,8,1,128,1,2,2048]{6,3,1,0,4,2,5:T(8,128)(2,1)}), bf16[2,8,1,128,1,2,2048]{6,3,1,0,4,2,5:T(8,128)(2,1)}, u32[]{:S(2)}, u32[]{:S(2)}) async-start(bf16[2,8,1,128,1,2,2048]{6,3,1,0,4,2,5:T(8,128)(2,1)} %copy.102), calls=%async_computation.2 | async-start | bytes 33554432 | tf_op jit(solution)/shard_map/all_to_all | solution.py:145
  1095.4 16.2 %copy-start = (bf16[1,32,64,2048]{3,1,2,0:T(8,128)(2,1)S(1)}, bf16[1,32,64,2048]{3,1,2,0:T(8,128)(2,1)}, u32[]{:S(2)}) copy-start(bf16[1,32,64,2048]{3,1,2,0:T(8,128)(2,1)} %get-tuple-element.23) | copy-start | bytes 25165828
  1095.4 16.2 %copy-start.1 = (bf16[1,32,64,2048]{3,1,2,0:T(8,128)(2,1)S(1)}, bf16[1,32,64,2048]{3,1,2,0:T(8,128)(2,1)}, u32[]{:S(2)}) copy-start(bf16[1,32,64,2048]{3,1,2,0:T(8,128)(2,1)} %get-tuple-element.24) | copy-start | bytes 25165828
  1224.9 24.6 %copy-start.4 = (f32[32,64]{1,0:T(8,128)S(1)}, f32[32,64]{1,0:T(8,128)}, u32[]{:S(2)}) copy-start(f32[32,64]{1,0:T(8,128)} %get-tuple-element.55) | copy-start | bytes 24580
  1224.9 24.6 %copy-start.5 = (f32[32,64]{1,0:T(8,128)S(1)}, f32[32,64]{1,0:T(8,128)}, u32[]{:S(2)}) copy-start(f32[32,64]{1,0:T(8,128)} %get-tuple-element.56) | copy-start | bytes 24580
  1262.5 6.8 copy-start.2
  1262.5 6.8 copy-start.3
where the time goes:
time: 1330 us; the launch traced here: 1320 us
  blocking collectives  369 us (28%)
  waiting for transfers between devices  307 us (23%)
  matrix products  282 us (21%)
  other arithmetic  178 us (13%)
  local copies, waits for them, and re-layouts  165 us (12%)
  starting transfers between devices  19.7 us (1%)
    all_to_all x1, blocking collectives, body(): lax.all_to_all(blocks, ('az', 'sec'), split_axis=4, concat_axis=1, tiled=...  369 us
    dot_general x10, matrix products, apply_table(): jnp.einsum(pattern, stacked, table, preferred_element_type=jnp.float32)  276 us
    all_to_all x1, waiting for transfers between devices, body(): lax.all_to_all(sectioned, 'sub', split_axis=1, concat_axis=3, tiled=True)  170 us
    all_to_all x1, waiting for transfers between devices, body(): lax.all_to_all(lax.all_to_all(blocks, ('az', 'sec'), split_axis=4, concat...  137 us
    another operation x5, other arithmetic  94.6 us
    another operation x2, local copies, waits for them, and re-layouts, body(): compressed.reshape(2, 1, 1, own_rows, outer_count, sub_count, RANGE // (o...  35.9 us
    sub x1, other arithmetic, product(): first_real * second_real - first_imag * second_imag  34.1 us
    all_to_all x1, local copies, waits for them, and re-layouts, body(): lax.all_to_all(sectioned, 'sub', split_axis=1, concat_axis=3, tiled=True)  30.9 us
  transfers between devices with their start and end apart: 2, of which 2 were waited for; matrix products, arithmetic and copies ran while one was open for 4% of the time, Pallas kernels for 0%

commit v1 on v0

v1 whole, which is shorter than its diff:
```python
import functools
import math

import jax
import jax.numpy as jnp
import numpy as np
from jax import lax
from jax.experimental import pallas as pl
from jax.experimental.pallas import tpu as pltpu
from jax.sharding import PartitionSpec as P

CHIRP = 2048
TAPS = 1024
PULSES = 2048
QUARTER = PULSES // 4
CHUNKS = 2


def azimuth_tables():
    j = np.arange(QUARTER)[:, None]
    b = np.arange(QUARTER)[None, :]
    tables = []
    for t in range(4):
        angles = -2.0 * math.pi / PULSES * ((b * (4 * j + t)) % PULSES)
        cosine, sine = np.cos(angles), np.sin(angles)
        tables.append(np.block([[cosine, -sine], [sine, cosine]]))
    return np.stack(tables).astype(np.float32).astype(jnp.bfloat16)


def toeplitz(taps, width):
    depth = CHIRP + width
    length = depth + width
    padded = jnp.pad(taps, (0, length - CHIRP))
    flat = jnp.tile(padded, width)[: width * (length - 1)]
    return flat.reshape(width, length - 1)[:, :depth].T


def range_kernel(width, order, echo_ref, real_ref, imag_ref, out_ref):
    start = pl.multiple_of(order(pl.program_id(0)) * width, width)
    depth = CHIRP + width
    both = jnp.dot(
        echo_ref[0, :, pl.ds(start, depth)], real_ref[...], preferred_element_type=jnp.float32
    ) + jnp.dot(
        echo_ref[1, :, pl.ds(start, depth)], imag_ref[...], preferred_element_type=jnp.float32
    )
    out_ref[0, 0, 0] = both[:, :width].astype(jnp.bfloat16)
    out_ref[0, 0, 1] = both[:, width:].astype(jnp.bfloat16)


def compress(
    extended, real_table, imag_table, chunk, chunks, sub_count, outer_count, own_bins
):
    rows = extended.shape[1]
    width = real_table.shape[1] // 2
    chunk_bins = own_bins // chunks
    per_chunk = chunk_bins // width
    per_dest = own_bins // width

    def order(step):
        return (step // per_chunk) * per_dest + chunk * per_chunk + step % per_chunk

    def place(step):
        dest = step // per_chunk
        return (dest % sub_count, dest // sub_count, 0, 0, step % per_chunk)

    whole = lambda *shape: pl.BlockSpec(
        shape, lambda step: (0,) * len(shape), pipeline_mode=pl.Buffered(1)
    )
    steps = outer_count * per_chunk
    return pl.pallas_call(
        functools.partial(range_kernel, width, order),
        grid=(steps,),
        in_specs=[
            whole(*extended.shape),
            whole(*real_table.shape),
            whole(*imag_table.shape),
        ],
        out_specs=pl.BlockSpec((1, 1, 2, rows, width), place),
        out_shape=jax.ShapeDtypeStruct(
            (sub_count, outer_count // sub_count, 2, rows, chunk_bins), jnp.bfloat16
        ),
        compiler_params=pltpu.CompilerParams(vmem_limit_bytes=48 * 1024 * 1024),
        cost_estimate=pl.CostEstimate(
            flops=steps * 4 * rows * real_table.shape[0] * 2 * width,
            bytes_accessed=2 * extended.size + 2 * steps * 2 * rows * width,
            transcendentals=0,
        ),
    )(extended, real_table, imag_table)


def turn(pair, count):
    real, imag = pair
    return ((real, imag), (-imag, real), (-real, -imag), (imag, -real))[count % 4]


def combine(pairs, direction, t):
    turned = [turn(pair, direction * a * t) for a, pair in enumerate(pairs)]
    real, imag = turned[0]
    for other_real, other_imag in turned[1:]:
        real, imag = real + other_real, imag + other_imag
    return real, imag


def azimuth_kernel(column_ref, replica_ref, count_ref, fwd_ref, inv_ref, out_ref):
    bins = out_ref.shape[-1]
    f32 = jnp.float32
    column = [column_ref[:, s].reshape(4, QUARTER, bins) for s in range(2)]
    column = [(column[0][a].astype(f32), column[1][a].astype(f32)) for a in range(4)]
    position = lax.broadcasted_iota(jnp.int32, (TAPS, bins), 0)
    kept = position < count_ref[...]
    taps = [jnp.where(kept, replica_ref[s].astype(f32), 0.0) for s in range(2)]
    taps = [
        (taps[0][a * QUARTER : (a + 1) * QUARTER], taps[1][a * QUARTER : (a + 1) * QUARTER])
        for a in range(TAPS // QUARTER)
    ]
    parts = []
    for t in range(4):
        sides = []
        for pieces in (column, taps):
            mixed = jnp.concatenate(combine(pieces, -1, t), axis=0).astype(jnp.bfloat16)
            found = jnp.dot(fwd_ref[t], mixed, preferred_element_type=f32)
            sides.append((found[:QUARTER], found[QUARTER:]))
        (x_real, x_imag), (q_real, q_imag) = sides
        y_real = (x_real * q_real + x_imag * q_imag) * (1.0 / PULSES)
        y_imag = (x_imag * q_real - x_real * q_imag) * (1.0 / PULSES)
        y = jnp.concatenate([y_real, y_imag], axis=0).astype(jnp.bfloat16)
        back = jnp.dot(inv_ref[t], y, preferred_element_type=f32)
        parts.append((back[:QUARTER], back[QUARTER:]))
    for a in range(4):
        real, imag = combine(parts, 1, a)
        out_ref[0, a * QUARTER : (a + 1) * QUARTER] = real.astype(jnp.bfloat16)
        out_ref[1, a * QUARTER : (a + 1) * QUARTER] = imag.astype(jnp.bfloat16)


def focus(columns, replicas, lengths, fwd, inv, chunk):
    outer_count, _, rows, chunk_bins = columns.shape
    width = min(256, chunk_bins)
    steps = chunk_bins // width
    shift = chunk * steps
    whole = lambda: pl.BlockSpec(
        fwd.shape, lambda step: (0, 0, 0), pipeline_mode=pl.Buffered(1)
    )
    return pl.pallas_call(
        azimuth_kernel,
        grid=(steps,),
        in_specs=[
            pl.BlockSpec((outer_count, 2, rows, width), lambda step: (0, 0, 0, step)),
            pl.BlockSpec((2, TAPS, width), lambda step: (0, 0, step + shift)),
            pl.BlockSpec((1, width), lambda step: (0, step + shift)),
            whole(),
            whole(),
        ],
        out_specs=pl.BlockSpec((2, PULSES, width), lambda step: (0, 0, step)),
        out_shape=jax.ShapeDtypeStruct((2, PULSES, chunk_bins), jnp.bfloat16),
        compiler_params=pltpu.CompilerParams(vmem_limit_bytes=58 * 1024 * 1024),
        cost_estimate=pl.CostEstimate(
            flops=steps * 4 * 2 * 1024 * 1024 * 3 * width,
            bytes_accessed=columns.size * 5 + 2 * fwd.size * 2,
            transcendentals=0,
        ),
    )(columns, replicas, lengths, fwd, inv)


def body(echoes, chirp_taps, replicas, lengths):
    sub_count = lax.axis_size("sub")
    outer_count = lax.axis_size(("az", "sec"))
    own_bins = replicas.shape[2]
    halo = lax.ppermute(
        echoes[:, :, :CHIRP],
        "sub",
        [(i, (i - 1) % sub_count) for i in range(sub_count)],
    )
    chunks = max(1, min(CHUNKS, own_bins // 128))
    width = min(256, own_bins // chunks)
    cosine = toeplitz(chirp_taps[0].astype(jnp.bfloat16), width)
    sine = toeplitz(chirp_taps[1].astype(jnp.bfloat16), width)
    real_table = jnp.concatenate([cosine, -sine], axis=1)
    imag_table = jnp.concatenate([sine, cosine], axis=1)
    fwd = jnp.asarray(azimuth_tables())
    inv = jnp.swapaxes(fwd, 1, 2)
    extended = jnp.concatenate([echoes, halo], axis=2)
    counts = lengths[None, :]
    crossed = []
    for chunk in range(chunks):
        pieces = compress(
            extended, real_table, imag_table, chunk, chunks, sub_count, outer_count, own_bins
        )
        crossed.append(lax.all_to_all(pieces, "sub", split_axis=0, concat_axis=0, tiled=True))
    results = []
    for chunk in range(chunks):
        pieces = crossed[chunk].reshape((outer_count,) + crossed[chunk].shape[2:])
        columns = lax.all_to_all(pieces, ("az", "sec"), split_axis=0, concat_axis=0, tiled=True)
        results.append(focus(columns, replicas, counts, fwd, inv, chunk))
    return jnp.concatenate(results, axis=2)


def solution(mesh):
    placed = (
        P(None, ("grp", "az", "sec"), "sub"),
        P(),
        P(None, None, ("grp", "az", "sec", "sub")),
        P(("grp", "az", "sec", "sub")),
    )
    return jax.shard_map(
        body,
        mesh=mesh,
        in_specs=placed,
        out_specs=P(None, None, ("grp", "az", "sec", "sub")),
        check_vma=False,
    )
```

time: 1330 us -> 750 us (0.56)
  matrix products: 282 us -> 0 us
  Pallas kernels: 0 us -> 201 us
  other arithmetic: 178 us -> 16.7 us
  local copies, waits for them, and re-layouts: 165 us -> 33.8 us
  waiting for transfers between devices: 307 us -> 191 us
  blocking collectives: 369 us -> 292 us
    dot_general x18 -> x0, matrix products: 282 us -> none  [the longest x10 276 us: apply_table(): jnp.einsum(pattern, stacked, table, preferred_element_type=jnp.float32)]
    pallas_call x0 -> x4, Pallas kernels: none -> 201 us  [the longest x2 106 us: compress(): pl.pallas_call(functools.partial(range_kernel, width, order), grid=(steps...]
    all_to_all x2, waiting for transfers between devices: 307 us -> 174 us  [the longest x1 136 us: body(): lax.all_to_all(pieces, ('az', 'sec'), split_axis=0, concat_axis=0, tiled=...]
    another operation x16 -> x1, other arithmetic: 125 us -> 0.72 us
    all_to_all x1 -> x2, blocking collectives: 369 us -> 292 us  [the longest x1 190 us: body(): lax.all_to_all(pieces, ('az', 'sec'), split_axis=0, concat_axis=0, tiled=...]
    another operation x3 -> x4, local copies, waits for them, and re-layouts: 63.9 us -> 3.28 us  [toeplitz(): flat = jnp.tile(padded, width)[:width * (length - 1)]]
    all_to_all x3 -> x0, local copies, waits for them, and re-layouts: 51.6 us -> none  [the longest x1 30.9 us: body(): lax.all_to_all(sectioned, 'sub', split_axis=1, concat_axis=3, tiled=True)]
    sub x1 -> x0, other arithmetic: 34.1 us -> none  [product(): first_real * second_real - first_imag * second_imag]
  transfers between devices with their start and end apart: 2 -> 3, of which waited for: 2 -> 3; matrix products, arithmetic and copies ran while one was open for 4% -> 4% of each run, Pallas kernels for 0% -> 13%
where the time goes in v1:
time: 750 us; the launch traced here: 749 us
  blocking collectives  292 us (39%)
  Pallas kernels  201 us (27%)
  waiting for transfers between devices  191 us (25%)
  local copies, waits for them, and re-layouts  33.8 us (5%)
  other arithmetic  16.7 us (2%)
  starting transfers between devices  15.2 us (2%)
    all_to_all x1, blocking collectives, body(): lax.all_to_all(pieces, ('az', 'sec'), split_axis=0, concat_axis=0, tiled=...  190 us
    all_to_all x1, waiting for transfers between devices, body(): lax.all_to_all(pieces, ('az', 'sec'), split_axis=0, concat_axis=0, tiled=...  136 us
    pallas_call x2, Pallas kernels, compress(): pl.pallas_call(functools.partial(range_kernel, width, order), grid=(steps...  106 us
    all_to_all x1, blocking collectives, body(): lax.all_to_all(pieces, 'sub', split_axis=0, concat_axis=0, tiled=True)  102 us
    pallas_call x2, Pallas kernels, focus(): pl.pallas_call(azimuth_kernel, grid=(steps,), in_specs=[pl.BlockSpec((out...  95.1 us
    all_to_all x1, waiting for transfers between devices, body(): lax.all_to_all(pieces, 'sub', split_axis=0, concat_axis=0, tiled=True)  37.5 us
    unnamed x7, local copies, waits for them, and re-layouts  19.3 us
    ppermute x1, waiting for transfers between devices, body(): lax.ppermute(echoes[:, :, :CHIRP], 'sub', [(i, (i - 1) % sub_count) for i...  17.2 us
  transfers between devices with their start and end apart: 3, of which 3 were waited for; matrix products, arithmetic and copies ran while one was open for 4% of the time, Pallas kernels for 13%

profile of v1, /device:TPU:0, one launch (start us, length us, event | category | flops | bytes accessed | tf_op | source)
XLA Modules:
  0.0 749.5 jit_solution(10919062295798729859)
XLA Ops:
  0.0 3.2 slice.23
  3.2 2.9 collective-permute-start
  6.1 0.7 convert.4
  6.8 0.1 slice_reduce_fusion.1
  6.9 0.1 tile.8
  7.0 1.5 tile.9
  8.5 1.8 reshape.16
  10.4 0.1 slice.32
  10.5 1.4 copy.8
  11.9 0.1 tile.20
  12.0 1.5 tile.21
  13.5 1.8 reshape.17
  15.4 1.1 slice.35
  16.5 1.6 copy.9
  18.1 0.1 bitcast_negate_fusion
  18.2 2.0 pad_maximum_fusion.2
  20.2 0.0 copy-start
  20.2 14.6 %constant_dynamic-update-slice_fusion.1 = bf16[2,256,18432]{2,1,0:T(8,128)(2,1)} fusion(bf16[2,256,16384]{2,1,0:T(8,128)(2,1)} %param.5), kind=kLoop, calls=%fused_computation.6 | loop fusion | bytes 33554432
  34.8 17.2 %collective-permute-done = bf16[2,256,2048]{2,1,0:T(8,128)(2,1)} collective-permute-done((bf16[2,256,2048]{2,1,0:T(8,128)(2,1)}, bf16[2,256,2048]{2,1,0:T(8,128)(2,1)}, u32[]{:S(2)}, u32[]{:S(2)}) %collective-permute-start) | collective-permute-done | bytes 2097184 | tf_op jit(solution)/shard_map/ppermute | solution.py:168
  52.0 3.2 constant_dynamic-update-slice_fusion.echo_ref
  55.2 0.0 copy-done
  55.2 52.9 %shard_map.57 = bf16[2,4,2,256,1024]{4,3,2,1,0:T(8,128)(2,1)} custom-call(bf16[2,256,18432]{2,1,0:T(8,128)(2,1)} %constant_dynamic-update-slice_fusion.echo_ref, bf16[2304,512]{1,0:T(8,128)(2,1)S(1)} %get-tuple-element.8.real_ref, bf16[2304,512]{1,0:T(8,128)(2,1)S(1)} %get-tuple-element.7.imag_ref), custom_call_target="tpu_custom_call" | custom-call | flops 38654705664 | bytes 27262976 | tf_op jit(solution)/shard_map/pallas_call | solution.py:70
  108.1 7.0 all-to-all-start.2
  115.1 0.0 copy-start.1
  115.1 1.7 copy-done.1
  116.7 52.9 %shard_map.55 = bf16[2,4,2,256,1024]{4,3,2,1,0:T(8,128)(2,1)} custom-call(bf16[2,256,18432]{2,1,0:T(8,128)(2,1)} %constant_dynamic-update-slice_fusion.echo_ref, bf16[2304,512]{1,0:T(8,128)(2,1)S(1)} %copy-done.1, bf16[2304,512]{1,0:T(8,128)(2,1)S(1)} %get-tuple-element.7.imag_ref), custom_call_target="tpu_custom_call" | custom-call | flops 38654705664 | bytes 27262976 | tf_op jit(solution)/shard_map/pallas_call | solution.py:70
  169.6 37.5 %all-to-all-done.2 = bf16[2,4,2,256,1024]{4,3,2,1,0:T(8,128)(2,1)} async-done(((bf16[2,4,2,256,1024]{4,3,2,1,0:T(8,128)(2,1)}), bf16[2,4,2,256,1024]{4,3,2,1,0:T(8,128)(2,1)}, u32[]{:S(2)}, u32[]{:S(2)}) %all-to-all-start.2) | async-done | bytes 8388640 | tf_op jit(solution)/shard_map/all_to_all | solution.py:188
  207.1 102.1 %all_to_all.20 = bf16[2,4,2,256,1024]{4,3,2,1,0:T(8,128)(2,1)} all-to-all(bf16[2,4,2,256,1024]{4,3,2,1,0:T(8,128)(2,1)} %shard_map.55), channel_id=1, replica_groups=mesh['grp'=2,'az'=4,'sec'=2,'sub'=2] {'sub'}, dimensions={0} | all-to-all | bytes 16777216 | tf_op jit(solution)/shard_map/all_to_all | solution.py:188
  309.3 189.8 %all_to_all.21.column_ref = bf16[8,2,256,1024]{3,2,1,0:T(8,128)(2,1)} all-to-all(bf16[8,2,256,1024]{3,2,1,0:T(8,128)(2,1)} %bitcast.4), channel_id=1, replica_groups=mesh['grp'=2,'az'=4,'sec'=2,'sub'=2] {'az','sec'}, dimensions={0} | all-to-all | bytes 16777216 | tf_op jit(solution)/shard_map/all_to_all | solution.py:192
  499.1 5.2 all-to-all-start.1
  504.3 47.6 %shard_map.58 = bf16[2,2048,1024]{2,1,0:T(8,128)(2,1)} custom-call(bf16[8,2,256,1024]{3,2,1,0:T(8,128)(2,1)} %all_to_all.21.column_ref, bf16[2,1024,2048]{2,1,0:T(8,128)(2,1)} %replica_ref.3, s32[1,2048]{1,0:T(1,128)} %bitcast.13, bf16[4,1024,1024]{2,1,0:T(8,128)(2,1)} %constant.5.clone.fwd_ref, bf16[4,1024,1024]{2,1,0:T(8,128)(2,1)} %constant.10.inv_ref), custom_call_target="tpu_custom_call" | custom-call | flops 25769803776 | bytes 37748736 | tf_op jit(solution)/shard_map/pallas_call | solution.py:143
  551.9 136.1 %all-to-all-done.1.column_ref = bf16[8,2,256,1024]{3,2,1,0:T(8,128)(2,1)} async-done(((bf16[8,2,256,1024]{3,2,1,0:T(8,128)(2,1)}), bf16[8,2,256,1024]{3,2,1,0:T(8,128)(2,1)}, u32[]{:S(2)}, u32[]{:S(2)}) %all-to-all-start.1) | async-done | bytes 8388640 | tf_op jit(solution)/shard_map/all_to_all | solution.py:192
  688.0 47.6 %shard_map.56 = bf16[2,2048,1024]{2,1,0:T(8,128)(2,1)} custom-call(bf16[8,2,256,1024]{3,2,1,0:T(8,128)(2,1)} %all-to-all-done.1.column_ref, bf16[2,1024,2048]{2,1,0:T(8,128)(2,1)} %replica_ref.3, s32[1,2048]{1,0:T(1,128)} %bitcast.14, bf16[4,1024,1024]{2,1,0:T(8,128)(2,1)} %constant.5.clone.fwd_ref, bf16[4,1024,1024]{2,1,0:T(8,128)(2,1)} %constant.10.inv_ref), custom_call_target="tpu_custom_call" | custom-call | flops 25769803776 | bytes 37748736 | tf_op jit(solution)/shard_map/pallas_call | solution.py:143
  735.6 13.9 %pad_maximum_fusion = bf16[2,2048,2048]{2,1,0:T(8,128)(2,1)} fusion(bf16[2,2048,1024]{2,1,0:T(8,128)(2,1)} %shard_map.58, bf16[2,2048,1024]{2,1,0:T(8,128)(2,1)} %shard_map.56), kind=kLoop, calls=%fused_computation | loop fusion | flops 33554432 | bytes 33554432 | tf_op jit(solution)/shard_map/concatenate | solution.py:194
  (2 shorter events, 0.0 us)
Async XLA Ops:
  3.2 48.9 %collective-permute-start = (bf16[2,256,2048]{2,1,0:T(8,128)(2,1)}, bf16[2,256,2048]{2,1,0:T(8,128)(2,1)}, u32[]{:S(2)}, u32[]{:S(2)}) collective-permute-start(bf16[2,256,2048]{2,1,0:T(8,128)(2,1)} %slice.23), channel_id=1, source_target_pairs={{0,1},{1,0},{2,3},{3,2},{4,5},{5,4},{6,7},{7,6},{8,9},{9,8},{10,11... | collective-permute-start | bytes 6291464 | tf_op jit(solution)/shard_map/ppermute | solution.py:168
  20.2 35.0 %copy-start = (bf16[2304,512]{1,0:T(8,128)(2,1)}, bf16[2304,512]{1,0:T(8,128)(2,1)S(1)}, u32[]{:S(2)}) copy-start(bf16[2304,512]{1,0:T(8,128)(2,1)S(1)} %get-tuple-element.8.real_ref) | copy-start | bytes 7077892
  108.1 99.1 %all-to-all-start.2 = ((bf16[2,4,2,256,1024]{4,3,2,1,0:T(8,128)(2,1)}), bf16[2,4,2,256,1024]{4,3,2,1,0:T(8,128)(2,1)}, u32[]{:S(2)}, u32[]{:S(2)}) async-start(bf16[2,4,2,256,1024]{4,3,2,1,0:T(8,128)(2,1)} %shard_map.57), calls=%async_computation.2 | async-start | bytes 16777216 | tf_op jit(solution)/shard_map/all_to_all | solution.py:188
  115.1 1.7 copy-start.1
  499.1 188.9 %all-to-all-start.1 = ((bf16[8,2,256,1024]{3,2,1,0:T(8,128)(2,1)}), bf16[8,2,256,1024]{3,2,1,0:T(8,128)(2,1)}, u32[]{:S(2)}, u32[]{:S(2)}) async-start(bf16[8,2,256,1024]{3,2,1,0:T(8,128)(2,1)} %bitcast.8), calls=%async_computation.1 | async-start | bytes 16777216 | tf_op jit(solution)/shard_map/all_to_all | solution.py:192

commit v2 on v1

--- a/solution.py
+++ b/solution.py
@@ -13,7 +13,7 @@
 TAPS = 1024
 PULSES = 2048
 QUARTER = PULSES // 4
-CHUNKS = 2
+CHUNKS = 4
 
 
 def azimuth_tables():
@@ -161,6 +161,21 @@
     )(columns, replicas, lengths, fwd, inv)
 
 
+def exchange(pieces, sub_count):
+    me = lax.axis_index("sub")
+    result = pieces
+    for step in range(1, sub_count):
+        target = lax.rem(me + step, sub_count)
+        source = lax.rem(me + sub_count - step, sub_count)
+        moved = lax.ppermute(
+            lax.dynamic_index_in_dim(pieces, target, 0),
+            "sub",
+            [(i, (i + step) % sub_count) for i in range(sub_count)],
+        )
+        result = lax.dynamic_update_slice_in_dim(result, moved, source, 0)
+    return result
+
+
 def body(echoes, chirp_taps, replicas, lengths):
     sub_count = lax.axis_size("sub")
     outer_count = lax.axis_size(("az", "sec"))
@@ -185,7 +200,7 @@
         pieces = compress(
             extended, real_table, imag_table, chunk, chunks, sub_count, outer_count, own_bins
         )
-        crossed.append(lax.all_to_all(pieces, "sub", split_axis=0, concat_axis=0, tiled=True))
+        crossed.append(exchange(pieces, sub_count))
     results = []
     for chunk in range(chunks):
         pieces = crossed[chunk].reshape((outer_count,) + crossed[chunk].shape[2:])

time: 750 us -> 581 us (0.77); the launches traced: 749 us -> 572 us
  blocking collectives: 292 us -> 0 us
  waiting for transfers between devices: 191 us -> 246 us
  Pallas kernels: 201 us -> 232 us
  local copies, waits for them, and re-layouts: 33.8 us -> 49.5 us
  starting transfers between devices: 15.2 us -> 28.5 us
    all_to_all x2 -> x0, blocking collectives: 292 us -> none  [the longest x1 190 us: body(): lax.all_to_all(pieces, ('az', 'sec'), split_axis=0, concat_axis=0, tiled=...]
    ppermute x0 -> x4, waiting for transfers between devices: none -> 184 us  [exchange(): lax.ppermute(lax.dynamic_index_in_dim(pieces, target, 0), 'sub', [(i, (i...]
    all_to_all x1 -> x4, waiting for transfers between devices: 136 us -> 42.7 us  [body(): lax.all_to_all(pieces, ('az', 'sec'), split_axis=0, concat_axis=0, tiled=...]
    all_to_all x1 -> x0, waiting for transfers between devices: 37.5 us -> none  [body(): lax.all_to_all(pieces, 'sub', split_axis=0, concat_axis=0, tiled=True)]
    pallas_call x2 -> x4, Pallas kernels: 95.1 us -> 113 us  [focus(): pl.pallas_call(azimuth_kernel, grid=(steps,), in_specs=[pl.BlockSpec((out...]
    pallas_call x2 -> x4, Pallas kernels: 106 us -> 120 us  [compress(): pl.pallas_call(functools.partial(range_kernel, width, order), grid=(steps...]
    all_to_all x1 -> x4, starting transfers between devices: 5.2 us -> 19 us  [body(): lax.all_to_all(pieces, ('az', 'sec'), split_axis=0, concat_axis=0, tiled=...]
    unnamed x7 -> x19, local copies, waits for them, and re-layouts: 19.3 us -> 23.6 us
  transfers between devices with their start and end apart: 3 -> 9, of which waited for: 3 -> 9; matrix products, arithmetic and copies ran while one was open for 4% -> 6% of each run, Pallas kernels for 13% -> 30%
where the time goes in v2:
time: 581 us; the launch traced here: 572 us
  waiting for transfers between devices  246 us (42%)
  Pallas kernels  232 us (40%)
  local copies, waits for them, and re-layouts  49.5 us (9%)
  starting transfers between devices  28.5 us (5%)
  other arithmetic  15.6 us (3%)
    ppermute x4, waiting for transfers between devices, exchange(): lax.ppermute(lax.dynamic_index_in_dim(pieces, target, 0), 'sub', [(i, (i...  184 us
    pallas_call x4, Pallas kernels, compress(): pl.pallas_call(functools.partial(range_kernel, width, order), grid=(steps...  120 us
    pallas_call x4, Pallas kernels, focus(): pl.pallas_call(azimuth_kernel, grid=(steps,), in_specs=[pl.BlockSpec((out...  113 us
    all_to_all x4, waiting for transfers between devices, body(): lax.all_to_all(pieces, ('az', 'sec'), split_axis=0, concat_axis=0, tiled=...  42.7 us
    unnamed x19, local copies, waits for them, and re-layouts  23.6 us
    all_to_all x4, starting transfers between devices, body(): lax.all_to_all(pieces, ('az', 'sec'), split_axis=0, concat_axis=0, tiled=...  19 us
    ppermute x1, waiting for transfers between devices, body(): lax.ppermute(echoes[:, :, :CHIRP], 'sub', [(i, (i - 1) % sub_count) for i...  18.8 us
    concatenate x1, other arithmetic, body(): return jnp.concatenate(results, axis=2)  12.4 us
  transfers between devices with their start and end apart: 9, of which 9 were waited for; matrix products, arithmetic and copies ran while one was open for 6% of the time, Pallas kernels for 30%

profile of v2, /device:TPU:0, one launch (start us, length us, event | category | flops | bytes accessed | tf_op | source)
XLA Modules:
  0.0 572.4 jit_solution(7429247117414895017)
XLA Ops:
  0.0 3.2 slice.23
  3.2 2.9 collective-permute-start
  6.3 1.5 tile.9
  7.8 1.8 reshape.22
  9.8 1.4 copy.8
  11.3 1.5 tile.21
  12.9 1.8 reshape.23
  15.4 1.1 bitcast_negate_fusion
  16.5 2.1 pad_maximum_fusion.2
  18.7 14.6 %constant_dynamic-update-slice_fusion.1 = bf16[2,256,18432]{2,1,0:T(8,128)(2,1)} fusion(bf16[2,256,16384]{2,1,0:T(8,128)(2,1)} %param.5), kind=kLoop, calls=%fused_computation.6 | loop fusion | bytes 33554432
  33.2 18.8 %collective-permute-done = bf16[2,256,2048]{2,1,0:T(8,128)(2,1)} collective-permute-done((bf16[2,256,2048]{2,1,0:T(8,128)(2,1)}, bf16[2,256,2048]{2,1,0:T(8,128)(2,1)}, u32[]{:S(2)}, u32[]{:S(2)}) %collective-permute-start) | collective-permute-done | bytes 2097184 | tf_op jit(solution)/shard_map/ppermute | solution.py:183
  52.1 3.2 constant_dynamic-update-slice_fusion.echo_ref
  55.2 29.9 %shard_map.61 = bf16[2,4,2,256,512]{4,3,2,1,0:T(8,128)(2,1)} custom-call(bf16[2,256,18432]{2,1,0:T(8,128)(2,1)} %constant_dynamic-update-slice_fusion.echo_ref, bf16[2304,512]{1,0:T(8,128)(2,1)S(1)} %get-tuple-element.8.real_ref, bf16[2304,512]{1,0:T(8,128)(2,1)S(1)} %get-tuple-element.7.imag_ref), custom_call_target="tpu_custom_call" | custom-call | flops 19327352832 | bytes 23068672 | tf_op jit(solution)/shard_map/pallas_call | solution.py:70
  85.2 2.0 constant_dynamic-slice_fusion
  87.2 1.8 collective-permute-start.4
  89.0 45.1 %collective-permute-done.4 = bf16[1,4,2,256,512]{4,3,2,1,0:T(8,128)(2,1)S(1)} collective-permute-done((bf16[1,4,2,256,512]{4,3,2,1,0:T(8,128)(2,1)S(1)}, bf16[1,4,2,256,512]{4,3,2,1,0:T(8,128)(2,1)S(1)}, u32[]{:S(2)}, u32[]{:S(2)}) %collective-permute-start.4) | collective-permute-done | bytes 2097184 | tf_op jit(solution)/shard_map/ppermute | solution.py:170
  134.3 2.0 copy-done.5
  136.3 4.8 all-to-all-start.3
  141.1 1.7 copy-done.1
  142.8 29.9 %shard_map.59 = bf16[2,4,2,256,512]{4,3,2,1,0:T(8,128)(2,1)} custom-call(bf16[2,256,18432]{2,1,0:T(8,128)(2,1)} %constant_dynamic-update-slice_fusion.echo_ref, bf16[2304,512]{1,0:T(8,128)(2,1)S(1)} %copy-done.1, bf16[2304,512]{1,0:T(8,128)(2,1)S(1)} %get-tuple-element.7.imag_ref), custom_call_target="tpu_custom_call" | custom-call | flops 19327352832 | bytes 23068672 | tf_op jit(solution)/shard_map/pallas_call | solution.py:70
  172.7 1.8 constant_dynamic-slice_fusion.1
  174.5 1.6 collective-permute-start.3
  176.1 46.5 %collective-permute-done.3 = bf16[1,4,2,256,512]{4,3,2,1,0:T(8,128)(2,1)S(1)} collective-permute-done((bf16[1,4,2,256,512]{4,3,2,1,0:T(8,128)(2,1)S(1)}, bf16[1,4,2,256,512]{4,3,2,1,0:T(8,128)(2,1)S(1)}, u32[]{:S(2)}, u32[]{:S(2)}) %collective-permute-start.3) | collective-permute-done | bytes 2097184 | tf_op jit(solution)/shard_map/ppermute | solution.py:170
  222.7 1.6 constant_dynamic-update-slice_fusion.3
  224.3 11.0 %all-to-all-done.3.column_ref = bf16[8,2,256,512]{3,2,1,0:T(8,128)(2,1)} async-done(((bf16[8,2,256,512]{3,2,1,0:T(8,128)(2,1)}), bf16[8,2,256,512]{3,2,1,0:T(8,128)(2,1)}, u32[]{:S(2)}, u32[]{:S(2)}) %all-to-all-start.3) | async-done | bytes 4194336 | tf_op jit(solution)/shard_map/all_to_all | solution.py:207
  235.2 5.1 all-to-all-start.2
  240.3 1.7 copy-done.2
  242.0 29.9 %shard_map.57 = bf16[2,4,2,256,512]{4,3,2,1,0:T(8,128)(2,1)} custom-call(bf16[2,256,18432]{2,1,0:T(8,128)(2,1)} %constant_dynamic-update-slice_fusion.echo_ref, bf16[2304,512]{1,0:T(8,128)(2,1)S(1)} %copy-done.2, bf16[2304,512]{1,0:T(8,128)(2,1)S(1)} %get-tuple-element.7.imag_ref), custom_call_target="tpu_custom_call" | custom-call | flops 19327352832 | bytes 23068672 | tf_op jit(solution)/shard_map/pallas_call | solution.py:70
  271.9 1.8 constant_dynamic-slice_fusion.2
  273.8 1.6 collective-permute-start.2
  275.3 46.5 %collective-permute-done.2 = bf16[1,4,2,256,512]{4,3,2,1,0:T(8,128)(2,1)S(1)} collective-permute-done((bf16[1,4,2,256,512]{4,3,2,1,0:T(8,128)(2,1)S(1)}, bf16[1,4,2,256,512]{4,3,2,1,0:T(8,128)(2,1)S(1)}, u32[]{:S(2)}, u32[]{:S(2)}) %collective-permute-start.2) | collective-permute-done | bytes 2097184 | tf_op jit(solution)/shard_map/ppermute | solution.py:170
  321.8 1.5 constant_dynamic-update-slice_fusion.4
  323.3 11.0 %all-to-all-done.2.column_ref = bf16[8,2,256,512]{3,2,1,0:T(8,128)(2,1)} async-done(((bf16[8,2,256,512]{3,2,1,0:T(8,128)(2,1)}), bf16[8,2,256,512]{3,2,1,0:T(8,128)(2,1)}, u32[]{:S(2)}, u32[]{:S(2)}) %all-to-all-start.2) | async-done | bytes 4194336 | tf_op jit(solution)/shard_map/all_to_all | solution.py:207
  334.3 4.6 all-to-all-start.1
  338.9 1.7 copy-done.3
  340.6 29.9 %shard_map.55 = bf16[2,4,2,256,512]{4,3,2,1,0:T(8,128)(2,1)} custom-call(bf16[2,256,18432]{2,1,0:T(8,128)(2,1)} %constant_dynamic-update-slice_fusion.echo_ref, bf16[2304,512]{1,0:T(8,128)(2,1)S(1)} %copy-done.3, bf16[2304,512]{1,0:T(8,128)(2,1)S(1)} %get-tuple-element.7.imag_ref), custom_call_target="tpu_custom_call" | custom-call | flops 19327352832 | bytes 23068672 | tf_op jit(solution)/shard_map/pallas_call | solution.py:70
  370.5 1.8 constant_dynamic-slice_fusion.3
  372.3 1.6 collective-permute-start.1
  373.9 46.4 %collective-permute-done.1 = bf16[1,4,2,256,512]{4,3,2,1,0:T(8,128)(2,1)S(1)} collective-permute-done((bf16[1,4,2,256,512]{4,3,2,1,0:T(8,128)(2,1)S(1)}, bf16[1,4,2,256,512]{4,3,2,1,0:T(8,128)(2,1)S(1)}, u32[]{:S(2)}, u32[]{:S(2)}) %collective-permute-start.1) | collective-permute-done | bytes 2097184 | tf_op jit(solution)/shard_map/ppermute | solution.py:170
  420.3 1.5 constant_dynamic-update-slice_fusion.5
  421.8 11.1 %all-to-all-done.1.column_ref = bf16[8,2,256,512]{3,2,1,0:T(8,128)(2,1)} async-done(((bf16[8,2,256,512]{3,2,1,0:T(8,128)(2,1)}), bf16[8,2,256,512]{3,2,1,0:T(8,128)(2,1)}, u32[]{:S(2)}, u32[]{:S(2)}) %all-to-all-start.1) | async-done | bytes 4194336 | tf_op jit(solution)/shard_map/all_to_all | solution.py:207
  432.9 4.5 all-to-all-start
  437.4 27.9 %shard_map.62 = bf16[2,2048,512]{2,1,0:T(8,128)(2,1)} custom-call(bf16[8,2,256,512]{3,2,1,0:T(8,128)(2,1)} %all-to-all-done.3.column_ref, bf16[2,1024,2048]{2,1,0:T(8,128)(2,1)} %replica_ref.7, s32[1,2048]{1,0:T(1,128)} %bitcast.15, bf16[4,1024,1024]{2,1,0:T(8,128)(2,1)} %constant.30.clone.fwd_ref, bf16[4,1024,1024]{2,1,0:T(8,128)(2,1)} %constant.35.inv_ref), custom_call_target="tpu_custom_call" | custom-call | flops 12884901888 | bytes 27262976 | tf_op jit(solution)/shard_map/pallas_call | solution.py:143
  465.4 28.2 %shard_map.60 = bf16[2,2048,512]{2,1,0:T(8,128)(2,1)} custom-call(bf16[8,2,256,512]{3,2,1,0:T(8,128)(2,1)} %all-to-all-done.2.column_ref, bf16[2,1024,2048]{2,1,0:T(8,128)(2,1)} %replica_ref.7, s32[1,2048]{1,0:T(1,128)} %bitcast.16, bf16[4,1024,1024]{2,1,0:T(8,128)(2,1)} %constant.30.clone.fwd_ref, bf16[4,1024,1024]{2,1,0:T(8,128)(2,1)} %constant.35.inv_ref), custom_call_target="tpu_custom_call" | custom-call | flops 12884901888 | bytes 27262976 | tf_op jit(solution)/shard_map/pallas_call | solution.py:143
  493.6 28.2 %shard_map.58 = bf16[2,2048,512]{2,1,0:T(8,128)(2,1)} custom-call(bf16[8,2,256,512]{3,2,1,0:T(8,128)(2,1)} %all-to-all-done.1.column_ref, bf16[2,1024,2048]{2,1,0:T(8,128)(2,1)} %replica_ref.7, s32[1,2048]{1,0:T(1,128)} %bitcast.17, bf16[4,1024,1024]{2,1,0:T(8,128)(2,1)} %constant.30.clone.fwd_ref, bf16[4,1024,1024]{2,1,0:T(8,128)(2,1)} %constant.35.inv_ref), custom_call_target="tpu_custom_call" | custom-call | flops 12884901888 | bytes 27262976 | tf_op jit(solution)/shard_map/pallas_call | solution.py:143
  521.8 9.7 %all-to-all-done.column_ref = bf16[8,2,256,512]{3,2,1,0:T(8,128)(2,1)} async-done(((bf16[8,2,256,512]{3,2,1,0:T(8,128)(2,1)}), bf16[8,2,256,512]{3,2,1,0:T(8,128)(2,1)}, u32[]{:S(2)}, u32[]{:S(2)}) %all-to-all-start) | async-done | bytes 4194336 | tf_op jit(solution)/shard_map/all_to_all | solution.py:207
  531.5 28.3 %shard_map.56 = bf16[2,2048,512]{2,1,0:T(8,128)(2,1)} custom-call(bf16[8,2,256,512]{3,2,1,0:T(8,128)(2,1)} %all-to-all-done.column_ref, bf16[2,1024,2048]{2,1,0:T(8,128)(2,1)} %replica_ref.7, s32[1,2048]{1,0:T(1,128)} %bitcast.18, bf16[4,1024,1024]{2,1,0:T(8,128)(2,1)} %constant.30.clone.fwd_ref, bf16[4,1024,1024]{2,1,0:T(8,128)(2,1)} %constant.35.inv_ref), custom_call_target="tpu_custom_call" | custom-call | flops 12884901888 | bytes 27262976 | tf_op jit(solution)/shard_map/pallas_call | solution.py:143
  559.8 12.4 %pad_maximum_fusion = bf16[2,2048,2048]{2,1,0:T(8,128)(2,1)} fusion(bf16[2,2048,512]{2,1,0:T(8,128)(2,1)S(1)} %copy-done.6, bf16[2,2048,512]{2,1,0:T(8,128)(2,1)} %shard_map.60, bf16[2,2048,512]{2,1,0:T(8,128)(2,1)} %shard_map.58, bf16[2,2048,512]{2,1,0:T(8,128)(2,1)} %shard_map.56), kind=kLoop, calls=%fused_computation | loop fusion | flops 67108864 | bytes 33554432 | tf_op jit(solution)/shard_map/concatenate | solution.py:209
  (22 shorter events, 1.3 us)
Async XLA Ops:
  0.0 6.1 %copy-start.7 = (f32[2,2048]{1,0:T(2,128)S(1)}, f32[2,2048]{1,0:T(2,128)}, u32[]{:S(2)}) copy-start(f32[2,2048]{1,0:T(2,128)} %param.6) | copy-start | bytes 49156
  3.2 48.9 %collective-permute-start = (bf16[2,256,2048]{2,1,0:T(8,128)(2,1)}, bf16[2,256,2048]{2,1,0:T(8,128)(2,1)}, u32[]{:S(2)}, u32[]{:S(2)}) collective-permute-start(bf16[2,256,2048]{2,1,0:T(8,128)(2,1)} %slice.23), channel_id=1, source_target_pairs={{0,1},{1,0},{2,3},{3,2},{4,5},{5,4},{6,7},{7,6},{8,9},{9,8},{10,11... | collective-permute-start | bytes 6291464 | tf_op jit(solution)/shard_map/ppermute | solution.py:183
  18.7 36.6 %copy-start = (bf16[2304,512]{1,0:T(8,128)(2,1)}, bf16[2304,512]{1,0:T(8,128)(2,1)S(1)}, u32[]{:S(2)}) copy-start(bf16[2304,512]{1,0:T(8,128)(2,1)S(1)} %get-tuple-element.8.real_ref) | copy-start | bytes 7077892
  85.2 48.9 %copy-start.4 = (bf16[2,4,2,256,512]{4,3,2,1,0:T(8,128)(2,1)S(1)}, bf16[2,4,2,256,512]{4,3,2,1,0:T(8,128)(2,1)}, u32[]{:S(2)}) copy-start(bf16[2,4,2,256,512]{4,3,2,1,0:T(8,128)(2,1)} %shard_map.61) | copy-start | bytes 12582916
  87.2 46.9 %collective-permute-start.4 = (bf16[1,4,2,256,512]{4,3,2,1,0:T(8,128)(2,1)S(1)}, bf16[1,4,2,256,512]{4,3,2,1,0:T(8,128)(2,1)S(1)}, u32[]{:S(2)}, u32[]{:S(2)}) collective-permute-start(bf16[1,4,2,256,512]{4,3,2,1,0:T(8,128)(2,1)S(1)} %constant_dynamic-slice_fusion), channel_id=1, source_target_pairs={{0,1},{1,0},{2,3},{3,2},{4,5},{5,4},{6,7},{7,6},{8,9},{9,8},{10,11... | collective-permute-start | bytes 6291464 | tf_op jit(solution)/shard_map/ppermute | solution.py:170
  134.3 2.0 copy-start.5
  136.3 98.9 %all-to-all-start.3 = ((bf16[8,2,256,512]{3,2,1,0:T(8,128)(2,1)}), bf16[8,2,256,512]{3,2,1,0:T(8,128)(2,1)}, u32[]{:S(2)}, u32[]{:S(2)}) async-start(bf16[8,2,256,512]{3,2,1,0:T(8,128)(2,1)} %bitcast.11), calls=%async_computation.3 | async-start | bytes 8388608 | tf_op jit(solution)/shard_map/all_to_all | solution.py:207
  141.1 1.7 copy-start.1
  174.5 48.1 %collective-permute-start.3 = (bf16[1,4,2,256,512]{4,3,2,1,0:T(8,128)(2,1)S(1)}, bf16[1,4,2,256,512]{4,3,2,1,0:T(8,128)(2,1)S(1)}, u32[]{:S(2)}, u32[]{:S(2)}) collective-permute-start(bf16[1,4,2,256,512]{4,3,2,1,0:T(8,128)(2,1)S(1)} %constant_dynamic-slice_fusion.1), channel_id=1, source_target_pairs={{0,1},{1,0},{2,3},{3,2},{4,5},{5,4},{6,7},{7,6},{8,9},{9,8},{10,11... | collective-permute-start | bytes 6291464 | tf_op jit(solution)/shard_map/ppermute | solution.py:170
  235.2 99.1 %all-to-all-start.2 = ((bf16[8,2,256,512]{3,2,1,0:T(8,128)(2,1)}), bf16[8,2,256,512]{3,2,1,0:T(8,128)(2,1)}, u32[]{:S(2)}, u32[]{:S(2)}) async-start(bf16[8,2,256,512]{3,2,1,0:T(8,128)(2,1)} %bitcast.5), calls=%async_computation.2 | async-start | bytes 8388608 | tf_op jit(solution)/shard_map/all_to_all | solution.py:207
  240.3 1.7 copy-start.2
  273.8 48.0 %collective-permute-start.2 = (bf16[1,4,2,256,512]{4,3,2,1,0:T(8,128)(2,1)S(1)}, bf16[1,4,2,256,512]{4,3,2,1,0:T(8,128)(2,1)S(1)}, u32[]{:S(2)}, u32[]{:S(2)}) collective-permute-start(bf16[1,4,2,256,512]{4,3,2,1,0:T(8,128)(2,1)S(1)} %constant_dynamic-slice_fusion.2), channel_id=1, source_target_pairs={{0,1},{1,0},{2,3},{3,2},{4,5},{5,4},{6,7},{7,6},{8,9},{9,8},{10,11... | collective-permute-start | bytes 6291464 | tf_op jit(solution)/shard_map/ppermute | solution.py:170
  334.3 98.6 %all-to-all-start.1 = ((bf16[8,2,256,512]{3,2,1,0:T(8,128)(2,1)}), bf16[8,2,256,512]{3,2,1,0:T(8,128)(2,1)}, u32[]{:S(2)}, u32[]{:S(2)}) async-start(bf16[8,2,256,512]{3,2,1,0:T(8,128)(2,1)} %bitcast.4), calls=%async_computation.1 | async-start | bytes 8388608 | tf_op jit(solution)/shard_map/all_to_all | solution.py:207
  338.9 1.7 copy-start.3
  372.3 48.0 %collective-permute-start.1 = (bf16[1,4,2,256,512]{4,3,2,1,0:T(8,128)(2,1)S(1)}, bf16[1,4,2,256,512]{4,3,2,1,0:T(8,128)(2,1)S(1)}, u32[]{:S(2)}, u32[]{:S(2)}) collective-permute-start(bf16[1,4,2,256,512]{4,3,2,1,0:T(8,128)(2,1)S(1)} %constant_dynamic-slice_fusion.3), channel_id=1, source_target_pairs={{0,1},{1,0},{2,3},{3,2},{4,5},{5,4},{6,7},{7,6},{8,9},{9,8},{10,11... | collective-permute-start | bytes 6291464 | tf_op jit(solution)/shard_map/ppermute | solution.py:170
  432.9 98.6 %all-to-all-start = ((bf16[8,2,256,512]{3,2,1,0:T(8,128)(2,1)}), bf16[8,2,256,512]{3,2,1,0:T(8,128)(2,1)}, u32[]{:S(2)}, u32[]{:S(2)}) async-start(bf16[8,2,256,512]{3,2,1,0:T(8,128)(2,1)} %bitcast.2), calls=%async_computation | async-start | bytes 8388608 | tf_op jit(solution)/shard_map/all_to_all | solution.py:207
  531.5 28.3 %copy-start.6 = (bf16[2,2048,512]{2,1,0:T(8,128)(2,1)S(1)}, bf16[2,2048,512]{2,1,0:T(8,128)(2,1)}, u32[]{:S(2)}) copy-start(bf16[2,2048,512]{2,1,0:T(8,128)(2,1)} %shard_map.62) | copy-start | bytes 12582916
